TPU v7x, 32 devices: a whole 2x2x4 slice. The times are simulated.
32 devices in a mesh: dp: 8 (over y, x, core), tensor: 4 (over z).
Axes of the slice: x: 2, y: 2, z: 4, core: 2. Of those that a mesh axis runs over, the one named last changes fastest.
Arguments:
- out_grad: bfloat16 [8, 256, 4096], P('dp', 'tensor'), may hold values from -6 to 6
- out_weight: bfloat16 [4096, 1024], P('dp', 'tensor'), may hold values from -0.1875 to 0.1875
- queries: bfloat16 [8, 256, 1024], P('dp', None, 'tensor'), may hold values from -5 to 5
- keys: bfloat16 [8, 256, 512], P('dp', None, 'tensor'), may hold values from -5 to 5, as said below
- values: bfloat16 [8, 256, 512], P('dp', None, 'tensor'), may hold values from -6 to 6, as said below
- segment_ids: int32 [8, 256], P('dp'), may hold values from 0 to 3, never falling along the last dimension, each value on 1 to 128 neighbouring positions
Outputs:
- d_queries: bfloat16 [8, 256, 1024], P('dp', None, 'tensor')
- d_keys: bfloat16 [8, 256, 512], P('dp', None, 'tensor')
- d_values: bfloat16 [8, 256, 512], P('dp', None, 'tensor')
- d_out_weight: float32 [4096, 1024], P('dp', 'tensor')
Inputs may be any that keep to these rules, and one draw needn't show every extreme that they name: `keys`: column blocks 2 g and 2 g + 1 are equal. `values`: column blocks 2 g and 2 g + 1 are equal.
All inputs are finite; a program needn't handle non-finite values.
Results may differ from a plain program's by a relative error of at most 0.018.
Values may be sent and summed in bfloat16 or wider, within the bound.
A program may use at most 128 MiB of HBM per device.

v0:
```python
import jax
import jax.numpy as jnp
from jax import lax
from jax.sharding import PartitionSpec as P

HD = 128


def from_partner(block, axis, bit):
    count = lax.axis_size(axis)
    route = []
    for low in range(count):
        high = low | 1 << bit
        if high != low and high < count:
            route += [(low, high), (high, low)]
    return lax.ppermute(block, axis, route)


def local(out_grad, out_weight, queries, keys, values, segment_ids):
    scale = HD ** (-0.5)
    grad_local = out_grad[0]
    query_rows = queries[0]
    length = query_rows.shape[0]
    width = query_rows.shape[1]
    heads_here = width // HD
    key_local = keys[0]
    value_local = values[0]
    query_heads = query_rows.reshape(length, heads_here, HD)
    scores = (
        jnp.einsum("qhd,kd->hqk", query_heads, key_local, preferred_element_type=jnp.float32)
        * scale
    )
    segments = segment_ids[0]
    position = jnp.arange(length)
    visible = (segments[:, None] == segments[None, :]) & (position[:, None] >= position[None, :])
    masked = jnp.where(visible[None], scores, -jnp.inf)
    top_score = jnp.max(masked, axis=-1, keepdims=True)
    raw_exp = jnp.exp(masked - top_score)
    attn_prob = raw_exp / jnp.sum(raw_exp, axis=-1, keepdims=True)
    prob_low = attn_prob.astype(jnp.bfloat16)
    attn_out = jnp.einsum(
        "hqk,kd->qhd", prob_low, value_local, preferred_element_type=jnp.float32
    ).astype(jnp.bfloat16)
    flat_out = attn_out.reshape(length, width)
    grad_full = lax.all_gather(grad_local, "tensor", axis=0, tiled=True)
    columns = grad_full
    grad_sum = jnp.dot(
        columns,
        lax.all_gather(out_weight, "dp", axis=0, tiled=True),
        preferred_element_type=jnp.float32,
    )
    columns = grad_full
    weight_rows = lax.psum_scatter(
        lax.dot_general(
            columns, flat_out, (((0,), (0,)), ((), ())), preferred_element_type=jnp.float32
        ).astype(jnp.bfloat16),
        "dp",
        scatter_dimension=0,
        tiled=True,
    ).astype(jnp.float32)
    grad_attn = grad_sum.astype(jnp.bfloat16)
    grad_heads = grad_attn.reshape(length, heads_here, HD)
    deltas = jnp.sum(grad_heads.astype(jnp.float32) * attn_out.astype(jnp.float32), axis=-1)
    grad_values = jnp.einsum(
        "hqk,qhd->kd", prob_low, grad_heads, preferred_element_type=jnp.float32
    )
    grad_prob = jnp.einsum(
        "qhd,kd->hqk", grad_heads, value_local, preferred_element_type=jnp.float32
    )
    grad_score = (attn_prob * (grad_prob - jnp.transpose(deltas)[:, :, None]) * scale).astype(
        jnp.bfloat16
    )
    grad_queries = jnp.einsum(
        "hqk,kd->qhd", grad_score, key_local, preferred_element_type=jnp.float32
    ).astype(jnp.bfloat16)
    grad_keys = jnp.einsum(
        "hqk,qhd->kd", grad_score, query_heads, preferred_element_type=jnp.float32
    )
    partner_keys, partner_values = (
        from_partner(grad_keys.astype(jnp.bfloat16), "tensor", 0).astype(grad_keys.dtype),
        from_partner(grad_values.astype(jnp.bfloat16), "tensor", 0).astype(grad_values.dtype),
    )
    keys_total = (grad_keys + partner_keys).astype(jnp.bfloat16)
    values_total = (grad_values + partner_values).astype(jnp.bfloat16)
    weight_grad = weight_rows / lax.axis_size("dp")
    return (
        grad_queries.reshape(1, length, width),
        keys_total[None],
        values_total[None],
        weight_grad,
    )


def solution(mesh):
    in_specs = (
        P("dp", "tensor", None),
        P("dp", "tensor"),
        P("dp", None, "tensor"),
        P("dp", None, "tensor"),
        P("dp", None, "tensor"),
        P("dp", None),
    )
    out_specs = (
        P("dp", None, "tensor"),
        P("dp", None, "tensor"),
        P("dp", None, "tensor"),
        P("dp", "tensor"),
    )
    return jax.shard_map(local, mesh=mesh, in_specs=in_specs, out_specs=out_specs, check_vma=False)
```

profile of v0, /device:TPU:0, one launch (start us, length us, event | category | flops | bytes accessed | tf_op | source)
XLA Modules:
  0.0 143.6 jit_solution(18421356278678418032)
XLA Ops:
  7.2 0.0 copy-start
  7.2 0.0 all-gather.6.cloned.1.call-start
  7.2 0.7 all-gather.6.cloned.1.call-update
  7.9 0.0 all-gather.4.cloned.1.call-start
  8.0 0.7 all-gather.4.cloned.1.call-update
  8.7 0.0 reduce-scatter.2.cloned.1.call-start
  8.7 0.9 reshape_squeeze.3
  9.7 0.9 fusion.16
  10.5 0.0 copy-done
  10.5 0.3 fusion.55
  10.9 47.4 %all-gather.6.cloned.1.call-done = bf16[1,256,4096]{2,1,0:T(8,128)(2,1)} async-done(((bf16[1,64,4096]{2,1,0:T(8,128)(2,1)}), bf16[1,256,4096]{2,1,0:T(8,128)(2,1)}) %all-gather.6.cloned.1.call-update) | async-done | bytes 2097168 | tf_op jit(solution)/shard_map/all_gather | solution.py:45
  58.3 28.5 %all-gather.4.cloned.1.call-done = bf16[4096,256]{1,0:T(8,128)(2,1)} async-done(((bf16[512,256]{1,0:T(8,128)(2,1)}), bf16[4096,256]{1,0:T(8,128)(2,1)}) %all-gather.4.cloned.1.call-update) | async-done | bytes 2097168 | tf_op jit(solution)/shard_map/all_gather | solution.py:49
  86.8 3.1 %fusion.13 = bf16[256,256]{0,1:T(8,128)(2,1)S(1)} fusion(bf16[4096,256]{1,0:T(8,128)(2,1)} %all-gather.4.cloned.1.call-done, bf16[1,256,4096]{2,1,0:T(8,128)(2,1)} %all-gather.6.cloned.1.call-done), kind=kOutput, calls=%fused_computation.18 | convolution fusion | flops 536936448 | bytes 4325376 | tf_op jit(solution)/shard_map/dot_general | solution.py:47
  89.9 0.0 copy-start.1
  90.0 0.5 multiply_reduce_fusion
  90.5 1.0 copy-done.1
  91.5 2.1 %fusion.1 = bf16[4096,256]{0,1:T(8,128)(2,1)} fusion(bf16[256,256]{0,1:T(8,128)(2,1)S(1)} %bitcast.105, bf16[1,256,4096]{2,1,0:T(8,128)(2,1)S(1)} %copy-done.1), kind=kOutput, calls=%fused_computation.2 | convolution fusion | flops 537919488 | bytes 4325376 | tf_op jit(solution)/shard_map/dot_general | solution.py:54
  93.6 0.0 reduce-scatter.2.cloned.1.call-update
  93.6 0.2 fusion.12
  93.8 0.2 fusion.64
  94.1 1.5 %collective-permute-start = (bf16[256,128]{1,0:T(8,128)(2,1)S(1)}, bf16[256,128]{1,0:T(8,128)(2,1)S(1)}, u32[]{:S(2)}, u32[]{:S(2)}) collective-permute-start(bf16[256,128]{1,0:T(8,128)(2,1)S(1)} %get-tuple-element.12), channel_id=1, source_target_pairs={{0,1},{1,0},{2,3},{3,2},{4,5},{5,4},{6,7},{7,6},{8,9},{9,8},{10,11... | collective-permute-start | bytes 196616 | tf_op jit(solution)/shard_map/ppermute | solution.py:16
  95.6 0.2 convolution_convert_fusion.1
  95.8 0.5 fusion.65
  96.4 0.8 copy.19
  97.1 0.5 collective-permute-start.1
  97.7 0.7 collective-permute-done
  98.4 0.6 fusion.20
  99.0 2.3 %collective-permute-done.1 = bf16[256,128]{1,0:T(8,128)(2,1)S(1)} collective-permute-done((bf16[256,128]{1,0:T(8,128)(2,1)S(1)}, bf16[256,128]{1,0:T(8,128)(2,1)S(1)}, u32[]{:S(2)}, u32[]{:S(2)}) %collective-permute-start.1) | collective-permute-done | bytes 65568 | tf_op jit(solution)/shard_map/ppermute | solution.py:16
  101.4 0.6 fusion.21
  102.0 33.0 %reduce-scatter.2.cloned.1.call-done = bf16[512,256]{0,1:T(8,128)(2,1)} async-done(((bf16[4096,256]{0,1:T(8,128)(2,1)}), bf16[512,256]{0,1:T(8,128)(2,1)}) %reduce-scatter.2.cloned.1.call-update) | async-done | bytes 262160 | tf_op jit(solution)/shard_map/reduce_scatter | solution.py:53
  135.0 1.0 convert_multiply_fusion
  136.0 1.0 copy.20
  (2 shorter events, 0.0 us)
Async XLA Ops:
  7.2 3.4 %copy-start = (bf16[1,256,128]{2,1,0:T(8,128)(2,1)S(1)}, bf16[1,256,128]{2,1,0:T(8,128)(2,1)}, u32[]{:S(2)}) copy-start(bf16[1,256,128]{2,1,0:T(8,128)(2,1)} %param.9) | copy-start | bytes 196612
  7.2 51.1 %all-gather.6.cloned.1.call-start = ((), (), s32[]{:S(2)}) async-start(), calls=%async_computation.3 | async-start | bytes 2621440 | tf_op jit(solution)/shard_map/all_gather | solution.py:45
  7.9 78.9 %all-gather.4.cloned.1.call-start = ((), (), s32[]{:S(2)}) async-start(), calls=%async_computation.1 | async-start | bytes 2359296 | tf_op jit(solution)/shard_map/all_gather | solution.py:49
  8.7 126.3 %reduce-scatter.2.cloned.1.call-start = ((), (), s32[]{:S(2)}) async-start(), calls=%async_computation.2 | async-start | bytes 2359296 | tf_op jit(solution)/shard_map/reduce_scatter | solution.py:53
  10.9 79.1 %copy-start.2 = (bf16[1,256,128]{2,1,0:T(8,128)(2,1)S(1)}, bf16[1,256,128]{2,1,0:T(8,128)(2,1)}, u32[]{:S(2)}) copy-start(bf16[1,256,128]{2,1,0:T(8,128)(2,1)} %param.10) | copy-start | bytes 196612
  89.9 1.6 %copy-start.1 = (bf16[1,256,4096]{2,1,0:T(8,128)(2,1)S(1)}, bf16[1,256,4096]{2,1,0:T(8,128)(2,1)}, u32[]{:S(2)}) copy-start(bf16[1,256,4096]{2,1,0:T(8,128)(2,1)} %all-gather.6.cloned.1.call-done) | copy-start | bytes 6291460
  94.1 4.3 %collective-permute-start = (bf16[256,128]{1,0:T(8,128)(2,1)S(1)}, bf16[256,128]{1,0:T(8,128)(2,1)S(1)}, u32[]{:S(2)}, u32[]{:S(2)}) collective-permute-start(bf16[256,128]{1,0:T(8,128)(2,1)S(1)} %get-tuple-element.12), channel_id=1, source_target_pairs={{0,1},{1,0},{2,3},{3,2},{4,5},{5,4},{6,7},{7,6},{8,9},{9,8},{10,11... | collective-permute-start | bytes 196616 | tf_op jit(solution)/shard_map/ppermute | solution.py:16
  97.1 4.3 %collective-permute-start.1 = (bf16[256,128]{1,0:T(8,128)(2,1)S(1)}, bf16[256,128]{1,0:T(8,128)(2,1)S(1)}, u32[]{:S(2)}, u32[]{:S(2)}) collective-permute-start(bf16[256,128]{1,0:T(8,128)(2,1)S(1)} %get-tuple-element.14), channel_id=1, source_target_pairs={{0,1},{1,0},{2,3},{3,2},{4,5},{5,4},{6,7},{7,6},{8,9},{9,8},{10,11... | collective-permute-start | bytes 196616 | tf_op jit(solution)/shard_map/ppermute | solution.py:16
Sparse Core Ops, SparseCore 0:
  9.6 48.6 all-gather.5
  60.1 26.5 all-gather.3
  93.7 41.2 reduce-scatter.1
where the time goes:
time: 144 us
  waiting for transfers between devices  113 us (78%)
  between operations  13.8 us (10%)
  matrix products  7.24 us (5%)
  local copies, waits for them, and re-layouts  3.77 us (3%)
  other arithmetic  3.15 us (2%)
  starting transfers between devices  2.2 us (2%)
    all_gather x1, waiting for transfers between devices, local(): grad_full = lax.all_gather(grad_local, 'tensor', axis=0, tiled=True)  47.4 us
    reduce_scatter x1, waiting for transfers between devices, local(): lax.psum_scatter(lax.dot_general(columns, flat_out, (((0,), (0,)), ((), (...  33 us
    all_gather x1, waiting for transfers between devices, local(): lax.all_gather(out_weight, 'dp', axis=0, tiled=True)  28.5 us
    dot_general x1, matrix products, local(): jnp.dot(columns, lax.all_gather(out_weight, 'dp', axis=0, tiled=True), pr...  3.15 us
    ppermute x2, waiting for transfers between devices, from_partner(): return lax.ppermute(block, axis, route)  3.08 us
  transfers between devices with their start and end apart: 5, of which 5 were waited for; matrix products, arithmetic and copies ran while one was open for 4% of the time, Pallas kernels for 0%

commit v1 on v0

--- a/solution.py
+++ b/solution.py
@@ -42,7 +42,15 @@
         "hqk,kd->qhd", prob_low, value_local, preferred_element_type=jnp.float32
     ).astype(jnp.bfloat16)
     flat_out = attn_out.reshape(length, width)
-    grad_full = lax.all_gather(grad_local, "tensor", axis=0, tiled=True)
+    n_dev = lax.axis_size("tensor")
+    current, pieces = (grad_local, [grad_local])
+    for _ in range(n_dev - 1):
+        current = lax.ppermute(current, "tensor", [(i, (i + 1) % n_dev) for i in range(n_dev)])
+        pieces.insert(0, current)
+    row_of_blocks = jnp.concatenate(pieces, axis=0)
+    grad_full = jnp.roll(
+        row_of_blocks, (lax.axis_index("tensor") + 1) * grad_local.shape[0], axis=0
+    )
     columns = grad_full
     grad_sum = jnp.dot(
         columns,

time: 144 us -> 126 us (0.88)
  waiting for transfers between devices: 113 us -> 85.4 us
  local copies, waits for them, and re-layouts: 3.77 us -> 8.42 us
  starting transfers between devices: 2.2 us -> 5.32 us
  matrix products: 7.24 us -> 8.86 us
    all_gather x1 -> x0, waiting for transfers between devices: 47.4 us -> none  [local(): grad_full = lax.all_gather(grad_local, 'tensor', axis=0, tiled=True)]
    ppermute x0 -> x3, waiting for transfers between devices: none -> 40.8 us  [local(): lax.ppermute(current, 'tensor', [(i, (i + 1) % n_dev) for i in range(n_de...]
    all_gather x1, waiting for transfers between devices: 28.5 us -> 8.6 us  [local(): lax.all_gather(out_weight, 'dp', axis=0, tiled=True)]
    unnamed x8 -> x14, local copies, waits for them, and re-layouts: 2.83 us -> 6.63 us
    ppermute x0 -> x3, starting transfers between devices: none -> 3.08 us  [local(): lax.ppermute(current, 'tensor', [(i, (i + 1) % n_dev) for i in range(n_de...]
    dot_general x1, matrix products: 2.06 us -> 3.69 us  [local(): lax.dot_general(columns, flat_out, (((0,), (0,)), ((), ())), preferred_el...]
  transfers between devices with their start and end apart: 5 -> 7, of which waited for: 5 -> 7; matrix products, arithmetic and copies ran while one was open for 4% -> 10% of each run, Pallas kernels for 0% -> 0%
where the time goes in v1:
time: 126 us
  waiting for transfers between devices  85.4 us (68%)
  between operations  14.2 us (11%)
  matrix products  8.86 us (7%)
  local copies, waits for them, and re-layouts  8.42 us (7%)
  starting transfers between devices  5.32 us (4%)
  other arithmetic  3.93 us (3%)
    ppermute x3, waiting for transfers between devices, local(): lax.ppermute(current, 'tensor', [(i, (i + 1) % n_dev) for i in range(n_de...  40.8 us
    reduce_scatter x1, waiting for transfers between devices, local(): lax.psum_scatter(lax.dot_general(columns, flat_out, (((0,), (0,)), ((), (...  33.6 us
    all_gather x1, waiting for transfers between devices, local(): lax.all_gather(out_weight, 'dp', axis=0, tiled=True)  8.6 us
    unnamed x14, local copies, waits for them, and re-layouts  6.63 us
    dot_general x1, matrix products, local(): lax.dot_general(columns, flat_out, (((0,), (0,)), ((), ())), preferred_el...  3.69 us
    dot_general x1, matrix products, local(): jnp.dot(columns, lax.all_gather(out_weight, 'dp', axis=0, tiled=True), pr...  3.15 us
    ppermute x3, starting transfers between devices, local(): lax.ppermute(current, 'tensor', [(i, (i + 1) % n_dev) for i in range(n_de...  3.08 us
  transfers between devices with their start and end apart: 7, of which 7 were waited for; matrix products, arithmetic and copies ran while one was open for 10% of the time, Pallas kernels for 0%

profile of v1, /device:TPU:0, one launch (start us, length us, event | category | flops | bytes accessed | tf_op | source)
XLA Modules:
  0.0 126.1 jit_solution(17779475500192312089)
XLA Ops:
  7.2 3.1 %collective-permute-start = (bf16[64,4096]{1,0:T(8,128)(2,1)}, bf16[64,4096]{1,0:T(8,128)(2,1)S(1)}, u32[]{:S(2)}, u32[]{:S(2)}) collective-permute-start(bf16[64,4096]{1,0:T(8,128)(2,1)} %bitcast.96), channel_id=1, source_target_pairs={{0,1},{1,2},{2,3},{3,0},{4,5},{5,6},{6,7},{7,4},{8,9},{9,10},{10,1... | collective-permute-start | bytes 1572872 | tf_op jit(solution)/shard_map/ppermute | solution.py:48
  10.3 14.2 %collective-permute-done = bf16[64,4096]{1,0:T(8,128)(2,1)S(1)} collective-permute-done((bf16[64,4096]{1,0:T(8,128)(2,1)}, bf16[64,4096]{1,0:T(8,128)(2,1)S(1)}, u32[]{:S(2)}, u32[]{:S(2)}) %collective-permute-start) | collective-permute-done | bytes 524320 | tf_op jit(solution)/shard_map/ppermute | solution.py:48
  24.5 14.9 %collective-permute-done.1 = bf16[64,4096]{1,0:T(8,128)(2,1)S(1)} collective-permute-done((bf16[64,4096]{1,0:T(8,128)(2,1)S(1)}, bf16[64,4096]{1,0:T(8,128)(2,1)S(1)}, u32[]{:S(2)}, u32[]{:S(2)}) %collective-permute-start.1) | collective-permute-done | bytes 524320 | tf_op jit(solution)/shard_map/ppermute | solution.py:48
  39.5 0.9 reshape_squeeze.3
  40.4 0.9 fusion.15
  41.3 0.4 fusion.56
  41.6 11.7 %collective-permute-done.2 = bf16[64,4096]{1,0:T(8,128)(2,1)S(1)} collective-permute-done((bf16[64,4096]{1,0:T(8,128)(2,1)S(1)}, bf16[64,4096]{1,0:T(8,128)(2,1)S(1)}, u32[]{:S(2)}, u32[]{:S(2)}) %collective-permute-start.2) | collective-permute-done | bytes 524320 | tf_op jit(solution)/shard_map/ppermute | solution.py:48
  53.4 0.8 constant_dynamic-update-slice_fusion.7
  54.2 0.8 constant_dynamic-update-slice_fusion.6
  55.0 0.9 constant_dynamic-update-slice_fusion.5
  55.9 0.8 constant_dynamic-update-slice_fusion.4
  56.7 0.8 constant_dynamic-update-slice_fusion.3
  57.6 0.8 constant_dynamic-update-slice_fusion.2
  58.4 0.8 constant_dynamic-update-slice_fusion.1
  59.2 0.8 constant_dynamic-update-slice_fusion
  60.1 8.6 %all-gather.2.cloned.1.call-done = bf16[4096,256]{1,0:T(8,128)(2,1)} async-done(((bf16[512,256]{1,0:T(8,128)(2,1)}), bf16[4096,256]{1,0:T(8,128)(2,1)}) %all-gather.2.cloned.1.call-update) | async-done | bytes 2097168 | tf_op jit(solution)/shard_map/all_gather | solution.py:57
  68.7 3.1 %fusion.12 = bf16[256,256]{0,1:T(8,128)(2,1)S(1)} fusion(bf16[4096,256]{1,0:T(8,128)(2,1)} %all-gather.2.cloned.1.call-done, bf16[512,4096]{1,0:T(8,128)(2,1)} %constant_dynamic-update-slice_fusion, s32[]{:T(128)S(6)} %select_n.19), kind=kOutput, calls=%fused_computation.17 | convolution fusion | flops 536936448 | bytes 4325380 | tf_op jit(solution)/shard_map/dot_general | solution.py:55
  71.8 0.5 multiply_reduce_fusion
  72.4 3.7 %convolution_convert_fusion = bf16[4096,256]{1,0:T(8,128)(2,1)} fusion(bf16[256,256]{0,1:T(8,128)(2,1)S(1)} %bitcast.100, bf16[512,4096]{1,0:T(8,128)(2,1)} %constant_dynamic-update-slice_fusion, s32[]{:T(128)S(6)} %select_n.19), kind=kOutput, calls=%fused_computation.1 | convolution fusion | flops 537919488 | bytes 4325380 | tf_op jit(solution)/shard_map/dot_general | solution.py:62
  76.1 0.5 fusion.66
  76.6 1.6 %collective-permute-start.4 = (bf16[256,128]{1,0:T(8,128)(2,1)S(1)}, bf16[256,128]{1,0:T(8,128)(2,1)S(1)}, u32[]{:S(2)}, u32[]{:S(2)}) collective-permute-start(bf16[256,128]{1,0:T(8,128)(2,1)S(1)} %get-tuple-element.14), channel_id=1, source_target_pairs={{0,1},{1,0},{2,3},{3,2},{4,5},{5,4},{6,7},{7,6},{8,9},{9,8},{10,11... | collective-permute-start | bytes 196616 | tf_op jit(solution)/shard_map/ppermute | solution.py:16
  78.1 0.2 fusion.11
  78.4 0.2 fusion.65
  78.6 0.2 convolution_convert_fusion.1
  78.8 0.6 collective-permute-start.3
  79.4 0.8 copy.19
  80.2 0.7 collective-permute-done.4
  80.9 0.6 fusion.20
  81.6 1.6 %collective-permute-done.3 = bf16[256,128]{1,0:T(8,128)(2,1)S(1)} collective-permute-done((bf16[256,128]{1,0:T(8,128)(2,1)S(1)}, bf16[256,128]{1,0:T(8,128)(2,1)S(1)}, u32[]{:S(2)}, u32[]{:S(2)}) %collective-permute-start.3) | collective-permute-done | bytes 65568 | tf_op jit(solution)/shard_map/ppermute | solution.py:16
  83.1 0.6 fusion.19
  83.8 33.6 %reduce-scatter.2.cloned.1.call-done = bf16[512,256]{1,0:T(8,128)(2,1)} async-done(((bf16[4096,256]{1,0:T(8,128)(2,1)}), bf16[512,256]{1,0:T(8,128)(2,1)}) %reduce-scatter.2.cloned.1.call-update) | async-done | bytes 262160 | tf_op jit(solution)/shard_map/reduce_scatter | solution.py:61
  117.4 1.8 %convert_multiply_fusion = f32[512,256]{1,0:T(8,128)} fusion(bf16[512,256]{1,0:T(8,128)(2,1)} %reduce-scatter.2.cloned.1.call-done), kind=kLoop, calls=%fused_computation.20 | loop fusion | flops 262144 | bytes 786432 | tf_op jit(solution)/shard_map/div | solution.py:93
  (12 shorter events, 0.1 us)
Async XLA Ops:
  7.2 34.1 %copy-start = (bf16[1,256,128]{2,1,0:T(8,128)(2,1)S(1)}, bf16[1,256,128]{2,1,0:T(8,128)(2,1)}, u32[]{:S(2)}) copy-start(bf16[1,256,128]{2,1,0:T(8,128)(2,1)} %param.9) | copy-start | bytes 196612
  7.2 48.7 %copy-start.1 = (bf16[1,64,4096]{2,1,0:T(8,128)(2,1)S(1)}, bf16[1,64,4096]{2,1,0:T(8,128)(2,1)}, u32[]{:S(2)}) copy-start(bf16[1,64,4096]{2,1,0:T(8,128)(2,1)} %param.6) | copy-start | bytes 1572868
  7.2 61.5 %all-gather.2.cloned.1.call-start = ((), (), s32[]{:S(2)}) async-start(), calls=%async_computation.1 | async-start | bytes 2359296 | tf_op jit(solution)/shard_map/all_gather | solution.py:57
  7.2 17.2 %collective-permute-start = (bf16[64,4096]{1,0:T(8,128)(2,1)}, bf16[64,4096]{1,0:T(8,128)(2,1)S(1)}, u32[]{:S(2)}, u32[]{:S(2)}) collective-permute-start(bf16[64,4096]{1,0:T(8,128)(2,1)} %bitcast.96), channel_id=1, source_target_pairs={{0,1},{1,2},{2,3},{3,0},{4,5},{5,6},{6,7},{7,4},{8,9},{9,10},{10,1... | collective-permute-start | bytes 1572872 | tf_op jit(solution)/shard_map/ppermute | solution.py:48
  24.5 14.9 %collective-permute-start.1 = (bf16[64,4096]{1,0:T(8,128)(2,1)S(1)}, bf16[64,4096]{1,0:T(8,128)(2,1)S(1)}, u32[]{:S(2)}, u32[]{:S(2)}) collective-permute-start(bf16[64,4096]{1,0:T(8,128)(2,1)S(1)} %collective-permute-done), channel_id=1, source_target_pairs={{0,1},{1,2},{2,3},{3,0},{4,5},{5,6},{6,7},{7,4},{8,9},{9,10},{10,1... | collective-permute-start | bytes 1572872 | tf_op jit(solution)/shard_map/ppermute | solution.py:48
  39.4 14.0 %collective-permute-start.2 = (bf16[64,4096]{1,0:T(8,128)(2,1)S(1)}, bf16[64,4096]{1,0:T(8,128)(2,1)S(1)}, u32[]{:S(2)}, u32[]{:S(2)}) collective-permute-start(bf16[64,4096]{1,0:T(8,128)(2,1)S(1)} %collective-permute-done.1), channel_id=1, source_target_pairs={{0,1},{1,2},{2,3},{3,0},{4,5},{5,6},{6,7},{7,4},{8,9},{9,10},{10,1... | collective-permute-start | bytes 1572872 | tf_op jit(solution)/shard_map/ppermute | solution.py:48
  39.4 78.0 %reduce-scatter.2.cloned.1.call-start = ((), (), s32[]{:S(2)}) async-start(), calls=%async_computation.2 | async-start | bytes 2359296 | tf_op jit(solution)/shard_map/reduce_scatter | solution.py:61
  56.7 15.1 %copy-start.2 = (bf16[1,256,128]{2,1,0:T(8,128)(2,1)S(1)}, bf16[1,256,128]{2,1,0:T(8,128)(2,1)}, u32[]{:S(2)}) copy-start(bf16[1,256,128]{2,1,0:T(8,128)(2,1)} %param.10) | copy-start | bytes 196612
  76.6 4.3 %collective-permute-start.4 = (bf16[256,128]{1,0:T(8,128)(2,1)S(1)}, bf16[256,128]{1,0:T(8,128)(2,1)S(1)}, u32[]{:S(2)}, u32[]{:S(2)}) collective-permute-start(bf16[256,128]{1,0:T(8,128)(2,1)S(1)} %get-tuple-element.14), channel_id=1, source_target_pairs={{0,1},{1,0},{2,3},{3,2},{4,5},{5,4},{6,7},{7,6},{8,9},{9,8},{10,11... | collective-permute-start | bytes 196616 | tf_op jit(solution)/shard_map/ppermute | solution.py:16
  78.8 4.3 %collective-permute-start.3 = (bf16[256,128]{1,0:T(8,128)(2,1)S(1)}, bf16[256,128]{1,0:T(8,128)(2,1)S(1)}, u32[]{:S(2)}, u32[]{:S(2)}) collective-permute-start(bf16[256,128]{1,0:T(8,128)(2,1)S(1)} %get-tuple-element.12), channel_id=1, source_target_pairs={{0,1},{1,0},{2,3},{3,2},{4,5},{5,4},{6,7},{7,6},{8,9},{9,8},{10,11... | collective-permute-start | bytes 196616 | tf_op jit(solution)/shard_map/ppermute | solution.py:16
Sparse Core Ops, SparseCore 0:
  39.5 29.1 all-gather.1
  76.2 41.1 reduce-scatter.1
